TPU v7x, 32 devices: a whole 2x2x4 slice. The times are simulated.
32 devices in a mesh: horiz: 16 (over z, y, core), vert: 2 (over x).
Axes of the slice: x: 2, y: 2, z: 4, core: 2. Of those that a mesh axis runs over, the one named last changes fastest.
Arguments:
- right_side: float32 [32, 64, 4096], P('vert', None, 'horiz'), may hold values from -6 to 6
- neighbours: int32 [4, 4096], P(None, 'horiz'), may hold values from 0 to 4095, as said below
- ocean_count: int32 [16], P('horiz'), may hold values from 64 to 256, as said below
- settling: float32 [32, 64], replicated, may hold values from 0.2 to 544
- coupling: float32 [32, 64, 64], P('vert'), may hold values from -0.3 to 0.3
- precond_inverse: float32 [32, 64, 64], P('vert'), may hold values from -1 to 1
Outputs:
- solution: float32 [32, 64, 4096], P('vert', None, 'horiz')
- residual: float32 [32, 64, 4096], P('vert', None, 'horiz')
Inputs may be any that keep to these rules, and one draw needn't show every extreme that they name: Each column's neighbours lie within 256 columns of it in the global order; in every tile but the first some column reads the column that lies 256 - 1 columns before the tile's first one, and the first column reads the column just before it; in every tile but the last some column reads the column that lies 256 - 1 columns after the tile's last one, and the last column reads the column just after it. Tile t has ocean_count[t] ocean columns, the first half (rounded up) at its start and the rest at its end; some tile is all ocean.
All inputs are finite; a program needn't handle non-finite values.
Results may differ from a plain program's by a relative error of at most 0.00018.
Values sent between devices are 32-bit elements; how exact they have to be, the bound alone decides.
A program may use at most 64 MiB of HBM per device.

v0:
```python
import jax
import jax.numpy as jnp
from jax import lax
from jax.sharding import PartitionSpec as P

RIM = 256
NB = 4


VERT_DIFFUSION = 0.5
HORIZ_DIFFUSION = 0.25
CENTER_VALUE = 1.0
HALF_WIDTH = 0.6


def with_halo(cells, sides, width):
    for axis, dim in sides:
        count = lax.axis_size(axis)
        ends = count - 1
        head = lax.slice_in_dim(cells, 0, width, axis=dim)
        tail = lax.slice_in_dim(cells, cells.shape[dim] - width, cells.shape[dim], axis=dim)
        cells = jnp.concatenate(
            [
                lax.ppermute(tail, axis, [(i, (i + 1) % count) for i in range(ends)]),
                cells,
                lax.ppermute(head, axis, [((i + 1) % count, i) for i in range(ends)]),
            ],
            axis=dim,
        )
    return cells


def shifted(block, axis, distance):
    devices = range(lax.axis_size(axis))
    route = [(i - distance, i) for i in devices if i - distance in devices]
    return lax.ppermute(block, axis, route)


def operate(field, coupling, diagonal, inflow_rate, local_index, ocean_mask):
    widened = with_halo(field, (("horiz", 2),), RIM)
    horizontal = jnp.zeros_like(field)
    for neighbour_slot in range(NB):
        horizontal = horizontal + jnp.take(widened, local_index[neighbour_slot], axis=2)
    stacked = with_halo(field, (("vert", 0),), 1)
    coupled = jnp.einsum(
        "kij,kjc->kic",
        coupling,
        field,
        precision=lax.Precision.HIGHEST,
        preferred_element_type=jnp.float32,
    )
    total = (
        diagonal[:, :, None] * field
        + coupled
        - inflow_rate[:, :, None] * stacked[:-2]
        - VERT_DIFFUSION * stacked[2:]
        - HORIZ_DIFFUSION * horizontal
    )
    return ocean_mask * total


def column_sweep(residual, blocks, inflow_rate):

    def column_one_level(previous, pieces):
        resid_level, block, rate = pieces
        current = jnp.dot(
            block,
            resid_level + rate[:, None] * previous,
            precision=lax.Precision.HIGHEST,
            preferred_element_type=jnp.float32,
        )
        return (current, current)

    _, swept = lax.scan(
        column_one_level, jnp.zeros_like(residual[0]), (residual, blocks, inflow_rate)
    )
    return swept


def chain_maps(blocks, inflow_rate):

    def chain_one_level(previous, pieces):
        block, rate = pieces
        current = jnp.dot(
            block,
            rate[:, None] * previous,
            precision=lax.Precision.HIGHEST,
            preferred_element_type=jnp.float32,
        )
        return (current, current)

    identity = jnp.eye(blocks.shape[1], dtype=jnp.float32)
    _, maps = lax.scan(chain_one_level, identity, (blocks, inflow_rate))
    return maps


def precondition(residual, blocks, inflow_rate):
    levels_here, classes, columns_here = residual.shape
    local_part = column_sweep(residual, blocks, inflow_rate)
    maps = chain_maps(blocks, inflow_rate)

    def relay_turn(turn_index, arriving):
        leaving = local_part[-1] + jnp.dot(
            maps[-1], arriving, precision=lax.Precision.HIGHEST, preferred_element_type=jnp.float32
        )
        return shifted(leaving, "vert", 1)

    inflow = lax.fori_loop(
        0, lax.axis_size("vert") - 1, relay_turn, jnp.zeros((classes, columns_here), jnp.float32)
    )
    carried = jnp.einsum(
        "kij,jc->kic",
        maps,
        inflow,
        precision=lax.Precision.HIGHEST,
        preferred_element_type=jnp.float32,
    )
    return local_part + carried


def body(right_side, neighbours, ocean_count, settling, coupling, precond_inverse):
    levels_here, classes, columns_here = right_side.shape
    level_start = lax.axis_index("vert") * levels_here
    column_start = lax.axis_index("horiz") * columns_here
    all_inflow = (
        jnp.concatenate([jnp.zeros_like(settling[:1]), settling[:-1]], axis=0) + VERT_DIFFUSION
    )
    inflow_rate = lax.dynamic_slice_in_dim(all_inflow, level_start, levels_here, 0)
    own_settling = lax.dynamic_slice_in_dim(settling, level_start, levels_here, 0)
    diagonal = 1.0 + own_settling + 2.0 * VERT_DIFFUSION + NB * HORIZ_DIFFUSION
    local_index = neighbours - column_start + RIM
    inside = jnp.arange(columns_here, dtype=jnp.int32)
    count_here = ocean_count[0]
    lower_part = (count_here + 1) // 2
    upper_part = count_here // 2
    ocean_flat = ((inside < lower_part) | (inside >= columns_here - upper_part)).astype(jnp.float32)
    ocean_mask = ocean_flat[None, None, :]
    source = right_side * ocean_mask
    spread_ratio = CENTER_VALUE / HALF_WIDTH
    ratio_first = 1.0 / spread_ratio
    ratio_second = 1.0 / (2.0 * spread_ratio - ratio_first)
    first_step = precondition(source, precond_inverse, inflow_rate) / CENTER_VALUE
    middle_residual = source - operate(
        first_step, coupling, diagonal, inflow_rate, local_index, ocean_mask
    )
    second_precond = precondition(middle_residual, precond_inverse, inflow_rate)
    second_step = (
        ratio_second * ratio_first * first_step + 2.0 * ratio_second / HALF_WIDTH * second_precond
    )
    solution = first_step + second_step
    residual = middle_residual - operate(
        second_step, coupling, diagonal, inflow_rate, local_index, ocean_mask
    )
    return (solution, residual)


def solution(mesh):
    in_specs = (
        P("vert", None, "horiz"),
        P(None, "horiz"),
        P("horiz"),
        P(),
        P("vert", None, None),
        P("vert", None, None),
    )
    out_specs = (P("vert", None, "horiz"), P("vert", None, "horiz"))
    return jax.shard_map(body, mesh=mesh, in_specs=in_specs, out_specs=out_specs, check_vma=False)
```

profile of v0, /device:TPU:14, one launch (start us, length us, event | category | flops | bytes accessed | tf_op | source)
XLA Modules:
  0.0 232.3 jit_solution(6589394413928968528)
XLA Ops:
  3.9 19.0 %while.8 = (s32[]{:T(128)}, f32[64,256]{1,0:T(8,128)S(1)}, f32[16,64,256]{2,1,0:T(8,128)S(1)}, f32[16,64,64]{2,1,0:T(8,128)}, f32[16,64,256]{2,1,0:T(8,128)}, /*index=5*/f32[16,64]{1,0:T(8,128)S(1)}, s32[]{:T(128)}) while((s32[]{:T(128)}, f32[64,256]{1,0:T(8,128)S(1)}, f32[16,64,256]{2,1,0:T(8,128)S(1)}, f32[16,64,64]{2,1,0:T(8,128)}, ...), condition=%wide.region_1.2_spmd, body=%wide.region_0.1_spmd.sunk | while | flops 12615682 | bytes 428625 | solution.py:74
  22.9 16.8 %while.9 = (s32[]{:T(128)}, f32[64,64]{1,0:T(8,128)S(1)}, f32[16,64,64]{2,1,0:T(8,128)S(1)}, f32[16,64,64]{2,1,0:T(8,128)}, f32[16,64]{1,0:T(8,128)S(1)}, /*index=5*/s32[]{:T(128)}) while((s32[]{:T(128)}, f32[64,64]{1,0:T(8,128)S(1)}, f32[16,64,64]{2,1,0:T(8,128)S(1)}, f32[16,64,64]{2,1,0:T(8,128)}, f32[16,64]{1,0:T(8,128)S(1)}, ...), condition=%wide.region_3.4_spmd, body=%wide.region_2.3_spmd.sunk | while | flops 3149826 | bytes 165961 | solution.py:93
  41.3 4.7 %collective-permute-done = f32[64,256]{1,0:T(8,128)S(1)} collective-permute-done((f32[64,256]{1,0:T(8,128)S(1)}, f32[64,256]{1,0:T(8,128)S(1)}, u32[]{:S(2)}, u32[]{:S(2)}) %collective-permute-start) | collective-permute-done | bytes 65568 | tf_op jit(solution)/shard_map/while/body/eval_jaxpr/ppermute | solution.py:36
  48.9 3.6 %collective-permute-start.4 = (f32[16,64,256]{2,1,0:T(8,128)S(1)}, f32[16,64,256]{2,1,0:T(8,128)S(1)}, u32[]{:S(2)}, u32[]{:S(2)}) collective-permute-start(f32[16,64,256]{2,1,0:T(8,128)S(1)} %convolution_add_fusion.1), channel_id=1, source_target_pairs={{2,0},{4,2},{6,4},{8,6},{10,8},{12,10},{14,12},{16,14},{18,16},{20... | collective-permute-start | bytes 3145736 | tf_op jit(solution)/shard_map/ppermute | solution.py:26
  53.9 4.5 %collective-permute-start.2 = (f32[1,64,256]{2,1,0:T(8,128)S(1)}, f32[1,64,256]{2,1,0:T(8,128)S(1)}, u32[]{:S(2)}, u32[]{:S(2)}) collective-permute-start(f32[1,64,256]{2,1,0:T(8,128)S(1)} %get-tuple-element.176), channel_id=1, source_target_pairs={{1,0},{3,2},{5,4},{7,6},{9,8},{11,10},{13,12},{15,14},{17,16},{19,... | collective-permute-start | bytes 196616 | tf_op jit(solution)/shard_map/ppermute | solution.py:26
  60.6 13.8 %collective-permute-done.3 = f32[16,64,256]{2,1,0:T(8,128)S(1)} collective-permute-done((f32[16,64,256]{2,1,0:T(8,128)S(1)}, f32[16,64,256]{2,1,0:T(8,128)S(1)}, u32[]{:S(2)}, u32[]{:S(2)}) %collective-permute-start.3) | collective-permute-done | bytes 1048608 | tf_op jit(solution)/shard_map/ppermute | solution.py:24
  76.4 6.9 %copy.8 = f32[16,64,768]{1,0,2:T(8,128)} copy(f32[16,64,768]{2,1,0:T(8,128)} %pad_maximum_fusion) | data formatting | bytes 6291456 | tf_op jit(solution)/shard_map/concatenate | solution.py:22
  83.3 4.9 %gather_fusion.1 = f32[256,16,64]{2,1,0:T(8,128)} fusion(f32[16,64,768]{1,0,2:T(8,128)} %copy.8, s32[1024]{0:T(1024)S(1)} %pad_clamp_fusion.2), kind=kCustom, calls=%fused_computation.1.clone | custom fusion | bytes 2098176 | tf_op jit(solution)/shard_map/jit(_take)/gather | solution.py:43
  88.2 3.6 %copy.11 = f32[256,16,64]{0,2,1:T(8,128)} copy(f32[256,16,64]{2,1,0:T(8,128)} %gather_fusion.1) | data formatting | bytes 2097152 | tf_op jit(solution)/shard_map/jit(_take)/gather | solution.py:43
  91.8 4.9 %gather_fusion.2 = f32[256,16,64]{2,1,0:T(8,128)} fusion(f32[16,64,768]{1,0,2:T(8,128)} %copy.8, s32[1024]{0:T(1024)S(1)} %pad_clamp_fusion.1), kind=kCustom, calls=%fused_computation.2.clone | custom fusion | bytes 2098176 | tf_op jit(solution)/shard_map/jit(_take)/gather | solution.py:43
  100.2 4.9 %gather_fusion = f32[256,16,64]{2,1,0:T(8,128)} fusion(f32[16,64,768]{1,0,2:T(8,128)} %copy.8, s32[1024]{0:T(1024)S(1)} %pad_clamp_fusion.3), kind=kCustom, calls=%fused_computation.clone | custom fusion | bytes 2098176 | tf_op jit(solution)/shard_map/jit(_take)/gather | solution.py:43
  108.6 4.9 %gather_fusion.3 = f32[256,16,64]{2,1,0:T(8,128)} fusion(f32[16,64,768]{1,0,2:T(8,128)} %copy.8, s32[1024]{0:T(1024)S(1)} %pad_clamp_fusion), kind=kCustom, calls=%fused_computation.3.clone | custom fusion | bytes 2098176 | tf_op jit(solution)/shard_map/jit(_take)/gather | solution.py:43
  121.6 26.9 %while.10 = (s32[]{:T(128)}, f32[64,256]{1,0:T(8,128)S(1)}, f32[16,64,256]{2,1,0:T(8,128)}, f32[16,64,64]{2,1,0:T(8,128)}, f32[16,64,256]{2,1,0:T(8,128)S(1)}, /*index=5*/f32[16,64]{1,0:T(8,128)S(1)}, s32[]{:T(128)}) while((s32[]{:T(128)}, f32[64,256]{1,0:T(8,128)S(1)}, f32[16,64,256]{2,1,0:T(8,128)}, f32[16,64,64]{2,1,0:T(8,128)}, ...), condition=%wide.region_5.7_spmd, body=%wide.region_4.6_spmd.sunk | while | flops 12615682 | bytes 428625 | solution.py:74
  150.7 4.8 %collective-permute-done.5 = f32[64,256]{1,0:T(8,128)S(1)} collective-permute-done((f32[64,256]{1,0:T(8,128)S(1)}, f32[64,256]{1,0:T(8,128)S(1)}, u32[]{:S(2)}, u32[]{:S(2)}) %collective-permute-start.5) | collective-permute-done | bytes 65568 | tf_op jit(solution)/shard_map/while/body/eval_jaxpr/ppermute | solution.py:36
  159.6 3.6 %collective-permute-start.9 = (f32[16,64,256]{2,1,0:T(8,128)S(1)}, f32[16,64,256]{2,1,0:T(8,128)S(1)}, u32[]{:S(2)}, u32[]{:S(2)}) collective-permute-start(f32[16,64,256]{2,1,0:T(8,128)S(1)} %multiply_add_fusion), channel_id=1, source_target_pairs={{2,0},{4,2},{6,4},{8,6},{10,8},{12,10},{14,12},{16,14},{18,16},{20... | collective-permute-start | bytes 3145736 | tf_op jit(solution)/shard_map/ppermute | solution.py:26
  164.6 4.7 %collective-permute-start.7 = (f32[1,64,256]{2,1,0:T(8,128)S(1)}, f32[1,64,256]{2,1,0:T(8,128)S(1)}, u32[]{:S(2)}, u32[]{:S(2)}) collective-permute-start(f32[1,64,256]{2,1,0:T(8,128)S(1)} %get-tuple-element.174), channel_id=1, source_target_pairs={{1,0},{3,2},{5,4},{7,6},{9,8},{11,10},{13,12},{15,14},{17,16},{19,... | collective-permute-start | bytes 196616 | tf_op jit(solution)/shard_map/ppermute | solution.py:26
  171.4 13.7 %collective-permute-done.8 = f32[16,64,256]{2,1,0:T(8,128)S(1)} collective-permute-done((f32[16,64,256]{2,1,0:T(8,128)S(1)}, f32[16,64,256]{2,1,0:T(8,128)S(1)}, u32[]{:S(2)}, u32[]{:S(2)}) %collective-permute-start.8) | collective-permute-done | bytes 1048608 | tf_op jit(solution)/shard_map/ppermute | solution.py:24
  187.1 6.9 %copy.16 = f32[16,64,768]{1,0,2:T(8,128)} copy(f32[16,64,768]{2,1,0:T(8,128)} %pad_maximum_fusion.1) | data formatting | bytes 6291456 | tf_op jit(solution)/shard_map/concatenate | solution.py:22
  194.0 4.8 %gather_fusion.4 = f32[256,16,64]{2,1,0:T(8,128)} fusion(f32[16,64,768]{1,0,2:T(8,128)} %copy.16, s32[1024]{0:T(1024)S(1)} %pad_clamp_fusion.3), kind=kCustom, calls=%fused_computation.4.clone | custom fusion | bytes 2098176 | tf_op jit(solution)/shard_map/jit(_take)/gather | solution.py:43
  198.8 4.9 %gather_fusion.5 = f32[256,16,64]{2,1,0:T(8,128)} fusion(f32[16,64,768]{1,0,2:T(8,128)} %copy.16, s32[1024]{0:T(1024)S(1)} %pad_clamp_fusion.2), kind=kCustom, calls=%fused_computation.5.clone | custom fusion | bytes 2098176 | tf_op jit(solution)/shard_map/jit(_take)/gather | solution.py:43
  203.7 4.9 %gather_fusion.6 = f32[256,16,64]{2,1,0:T(8,128)} fusion(f32[16,64,768]{1,0,2:T(8,128)} %copy.16, s32[1024]{0:T(1024)S(1)} %pad_clamp_fusion.1), kind=kCustom, calls=%fused_computation.6.clone | custom fusion | bytes 2098176 | tf_op jit(solution)/shard_map/jit(_take)/gather | solution.py:43
  208.6 4.9 %gather_fusion.7 = f32[256,16,64]{2,1,0:T(8,128)} fusion(f32[16,64,768]{1,0,2:T(8,128)} %copy.16, s32[1024]{0:T(1024)S(1)} %pad_clamp_fusion), kind=kCustom, calls=%fused_computation.7.clone | custom fusion | bytes 2098176 | tf_op jit(solution)/shard_map/jit(_take)/gather | solution.py:43
  213.6 3.5 %copy.17 = f32[256,16,64]{0,2,1:T(8,128)} copy(f32[256,16,64]{2,1,0:T(8,128)} %gather_fusion.4) | data formatting | bytes 2097152 | tf_op jit(solution)/shard_map/jit(_take)/gather | solution.py:43
  227.5 4.8 %fusion.29 = (f32[16,64,256]{2,1,0:T(8,128)}, f32[16,64,256]{2,1,0:T(8,128)}) fusion(f32[16,64,256]{2,1,0:T(8,128)} %copy-done.1, f32[1,64,256]{2,1,0:T(8,128)S(1)} %collective-permute-done.7, f32[16,64,256]{2,1,0:T(8,128)S(1)} %multiply_add_fusion, f32[16,64,256]{2,1,0:T(8,128)} %fusion.23, f32[1,64,256]{2,1,0:T(8,128)S(1)} %collective-permute-done.6, ...), kind=kLoop, calls=%fused_computation.52 | loop fusion | flops 4718592 | bytes 10622976 | tf_op jit(solution)/shard_map/sub | solution.py:151
  (203 shorter events, 110.7 us)
Async XLA Ops:
  0.6 57.9 %copy-start = (f32[16,64,64]{2,1,0:T(8,128)S(1)}, f32[16,64,64]{2,1,0:T(8,128)}, u32[]{:S(2)}) copy-start(f32[16,64,64]{2,1,0:T(8,128)} %param.18) | copy-start | bytes 786436
  0.6 3.1 %copy-start.2 = (f32[32,64]{1,0:T(8,128)S(1)}, f32[32,64]{1,0:T(8,128)}, u32[]{:S(2)}) copy-start(f32[32,64]{1,0:T(8,128)} %param.17) | copy-start | bytes 24580
  3.9 37.3 %copy-start.3 = (s32[4,256]{1,0:T(4,128)S(1)}, s32[4,256]{1,0:T(4,128)}, u32[]{:S(2)}) copy-start(s32[4,256]{1,0:T(4,128)} %param.15) | copy-start | bytes 12292
  39.9 6.2 %collective-permute-start = (f32[64,256]{1,0:T(8,128)S(1)}, f32[64,256]{1,0:T(8,128)S(1)}, u32[]{:S(2)}, u32[]{:S(2)}) collective-permute-start(f32[64,256]{1,0:T(8,128)S(1)} %get-tuple-element.181), channel_id=1, source_target_pairs={{0,1},{2,3},{4,5},{6,7},{8,9},{10,11},{12,13},{14,15},{16,17},{18,... | collective-permute-start | bytes 196616 | tf_op jit(solution)/shard_map/while/body/eval_jaxpr/ppermute | solution.py:36
  47.0 27.4 %collective-permute-start.3 = (f32[16,64,256]{2,1,0:T(8,128)S(1)}, f32[16,64,256]{2,1,0:T(8,128)S(1)}, u32[]{:S(2)}, u32[]{:S(2)}) collective-permute-start(f32[16,64,256]{2,1,0:T(8,128)S(1)} %convolution_add_fusion.1), channel_id=1, source_target_pairs={{0,2},{2,4},{4,6},{6,8},{8,10},{10,12},{12,14},{14,16},{16,18},{18... | collective-permute-start | bytes 3145736 | tf_op jit(solution)/shard_map/ppermute | solution.py:24
  48.9 25.4 %collective-permute-start.4 = (f32[16,64,256]{2,1,0:T(8,128)S(1)}, f32[16,64,256]{2,1,0:T(8,128)S(1)}, u32[]{:S(2)}, u32[]{:S(2)}) collective-permute-start(f32[16,64,256]{2,1,0:T(8,128)S(1)} %convolution_add_fusion.1), channel_id=1, source_target_pairs={{2,0},{4,2},{6,4},{8,6},{10,8},{12,10},{14,12},{16,14},{18,16},{20... | collective-permute-start | bytes 3145736 | tf_op jit(solution)/shard_map/ppermute | solution.py:26
  52.6 64.3 %collective-permute-start.1 = (f32[1,64,256]{2,1,0:T(8,128)S(1)}, f32[1,64,256]{2,1,0:T(8,128)S(1)}, u32[]{:S(2)}, u32[]{:S(2)}) collective-permute-start(f32[1,64,256]{2,1,0:T(8,128)S(1)} %get-tuple-element.175), channel_id=1, source_target_pairs={{0,1},{2,3},{4,5},{6,7},{8,9},{10,11},{12,13},{14,15},{16,17},{18,... | collective-permute-start | bytes 196616 | tf_op jit(solution)/shard_map/ppermute | solution.py:24
  53.9 63.0 %collective-permute-start.2 = (f32[1,64,256]{2,1,0:T(8,128)S(1)}, f32[1,64,256]{2,1,0:T(8,128)S(1)}, u32[]{:S(2)}, u32[]{:S(2)}) collective-permute-start(f32[1,64,256]{2,1,0:T(8,128)S(1)} %get-tuple-element.176), channel_id=1, source_target_pairs={{1,0},{3,2},{5,4},{7,6},{9,8},{11,10},{13,12},{15,14},{17,16},{19,... | collective-permute-start | bytes 196616 | tf_op jit(solution)/shard_map/ppermute | solution.py:26
  148.5 2.2 copy-start.1
  149.4 6.2 %collective-permute-start.5 = (f32[64,256]{1,0:T(8,128)S(1)}, f32[64,256]{1,0:T(8,128)S(1)}, u32[]{:S(2)}, u32[]{:S(2)}) collective-permute-start(f32[64,256]{1,0:T(8,128)S(1)} %bitcast_add_fusion.10), channel_id=1, source_target_pairs={{0,1},{2,3},{4,5},{6,7},{8,9},{10,11},{12,13},{14,15},{16,17},{18,... | collective-permute-start | bytes 196616 | tf_op jit(solution)/shard_map/while/body/eval_jaxpr/ppermute | solution.py:36
  157.7 27.4 %collective-permute-start.8 = (f32[16,64,256]{2,1,0:T(8,128)S(1)}, f32[16,64,256]{2,1,0:T(8,128)S(1)}, u32[]{:S(2)}, u32[]{:S(2)}) collective-permute-start(f32[16,64,256]{2,1,0:T(8,128)S(1)} %multiply_add_fusion), channel_id=1, source_target_pairs={{0,2},{2,4},{4,6},{6,8},{8,10},{10,12},{12,14},{14,16},{16,18},{18... | collective-permute-start | bytes 3145736 | tf_op jit(solution)/shard_map/ppermute | solution.py:24
  159.6 25.4 %collective-permute-start.9 = (f32[16,64,256]{2,1,0:T(8,128)S(1)}, f32[16,64,256]{2,1,0:T(8,128)S(1)}, u32[]{:S(2)}, u32[]{:S(2)}) collective-permute-start(f32[16,64,256]{2,1,0:T(8,128)S(1)} %multiply_add_fusion), channel_id=1, source_target_pairs={{2,0},{4,2},{6,4},{8,6},{10,8},{12,10},{14,12},{16,14},{18,16},{20... | collective-permute-start | bytes 3145736 | tf_op jit(solution)/shard_map/ppermute | solution.py:26
  163.3 64.2 %collective-permute-start.6 = (f32[1,64,256]{2,1,0:T(8,128)S(1)}, f32[1,64,256]{2,1,0:T(8,128)S(1)}, u32[]{:S(2)}, u32[]{:S(2)}) collective-permute-start(f32[1,64,256]{2,1,0:T(8,128)S(1)} %get-tuple-element.173), channel_id=1, source_target_pairs={{0,1},{2,3},{4,5},{6,7},{8,9},{10,11},{12,13},{14,15},{16,17},{18,... | collective-permute-start | bytes 196616 | tf_op jit(solution)/shard_map/ppermute | solution.py:24
  164.6 62.9 %collective-permute-start.7 = (f32[1,64,256]{2,1,0:T(8,128)S(1)}, f32[1,64,256]{2,1,0:T(8,128)S(1)}, u32[]{:S(2)}, u32[]{:S(2)}) collective-permute-start(f32[1,64,256]{2,1,0:T(8,128)S(1)} %get-tuple-element.174), channel_id=1, source_target_pairs={{1,0},{3,2},{5,4},{7,6},{9,8},{11,10},{13,12},{15,14},{17,16},{19,... | collective-permute-start | bytes 196616 | tf_op jit(solution)/shard_map/ppermute | solution.py:26
where the time goes:
time: 236 us; the launch traced here: 232 us
  local copies, waits for them, and re-layouts  82.8 us (35%)
  matrix products  68.2 us (29%)
  waiting for transfers between devices  37 us (16%)
  starting transfers between devices  25.6 us (11%)
  other arithmetic  15.7 us (7%)
    gather x16, local copies, waits for them, and re-layouts, operate(): jnp.take(widened, local_index[neighbour_slot], axis=2)  67.2 us
    dot_general x32, matrix products, column_one_level(): jnp.dot(block, resid_level + rate[:, None] * previous, precision=lax.Prec...  44.8 us
    ppermute x4, waiting for transfers between devices, with_halo(): lax.ppermute(tail, axis, [(i, (i + 1) % count) for i in range(ends)])  27.4 us
    ppermute x4, starting transfers between devices, with_halo(): lax.ppermute(head, axis, [((i + 1) % count, i) for i in range(ends)])  16.6 us
    dot_general x16, matrix products, chain_one_level(): jnp.dot(block, rate[:, None] * previous, precision=lax.Precision.HIGHEST,...  15.9 us
    concatenate x2, local copies, waits for them, and re-layouts, with_halo(): jnp.concatenate([lax.ppermute(tail, axis, [(i, (i + 1) % count) for i in...  13.7 us
    ppermute x2, waiting for transfers between devices, shifted(): return lax.ppermute(block, axis, route)  9.56 us
    ppermute x4, starting transfers between devices, with_halo(): lax.ppermute(tail, axis, [(i, (i + 1) % count) for i in range(ends)])  6.43 us
  transfers between devices with their start and end apart: 10, of which 4 were waited for; matrix products, arithmetic and copies ran while one was open for 38% of the time, Pallas kernels for 0%

commit v1 on v0

v1 whole, which is shorter than its diff:
```python
import jax
import jax.numpy as jnp
from jax import lax
from jax.experimental import pallas as pl
from jax.experimental.pallas import tpu as pltpu
from jax.sharding import PartitionSpec as P

VERT_DIFFUSION = 0.5
HORIZ_DIFFUSION = 0.25
HALF_WIDTH = 0.6
NB = 4
SPREAD = 1.0 / HALF_WIDTH
RATIO_FIRST = 1.0 / SPREAD
RATIO_SECOND = 1.0 / (2.0 * SPREAD - RATIO_FIRST)
CA = RATIO_SECOND * RATIO_FIRST
CB = 2.0 * RATIO_SECOND / HALF_WIDTH

F32 = jnp.float32
BF = jnp.bfloat16
CHUNKS = 4


def split(x):
    hi = x.astype(BF)
    return hi, (x - hi.astype(F32)).astype(BF)


def mm(a, b):
    return jnp.dot(a, b, preferred_element_type=F32)


def mm3(ahi, alo, bhi, blo):
    return mm(ahi, bhi) + mm(ahi, blo) + mm(alo, bhi)


def make_kernel(tiles, slabs, levels, classes, cols):
    rows = levels * classes
    part = rows // CHUNKS
    block = 256

    def kernel(rhs, nbr, count, binv, coup, rate_row, diag, rate, sol, res,
               win, info, info_adj, h1, g_own, g_adj, phi, plo, xhi, xlo, fbuf, fout, mid,
               pbuf, pout, sbuf,
               recv, send_mate, send_direct, send_fwd, info_s, info_r, h_s, h_r, v_s, v_r):
        t = lax.axis_index("horiz")
        v = lax.axis_index("vert")
        c = lax.rem(t, 2)
        j = lax.div(t, 2)
        odd = lax.rem(j, 2)
        inner = lax.rem(j + c, 2) == 1
        own = 2 - c
        mate_pos = 3 - 3 * c
        mate = t + 1 - 2 * c
        direct = jnp.where(odd == 0, 2 * j + 2, 2 * j - 1)
        fwd = jnp.where(odd == 0, 2 * j + 4, 2 * j - 3)
        has_fwd = jnp.logical_and(inner, jnp.logical_and(fwd >= 0, fwd < tiles))
        adj = t - 1 + 2 * c
        has_adj = jnp.logical_and(adj >= 0, adj < tiles)
        first_slab = v == 0
        last_slab = v == slabs - 1

        def remote(src, dst, s, r, to):
            return pltpu.make_async_remote_copy(
                src_ref=src, dst_ref=dst, send_sem=s, recv_sem=r, device_id=to,
                device_id_type=pl.DeviceIdType.MESH)

        def piece(pos, ch):
            return win.at[pos, pl.ds(ch * part, part)]

        inside = lax.broadcasted_iota(jnp.int32, (1, cols), 1)
        n = count[0]
        low = lax.div(n + 1, 2)
        high = cols - lax.div(n, 2)
        ocean = jnp.logical_or(inside < low, inside >= high)
        ocean_i = ocean.astype(jnp.int32)
        ocean_f = ocean.astype(F32)
        info[...] = jnp.concatenate([nbr[...], jnp.broadcast_to(ocean_i, (4, cols))], axis=0)
        adj_copy = remote(info, info_adj, info_s, info_r, {"horiz": adj})

        @pl.when(has_adj)
        def _():
            adj_copy.start()

        directs = []
        for ch in range(CHUNKS):
            r = pl.ds(ch * part, part)
            win[own, r] = rhs[r] * ocean_f
            cp = remote(piece(own, ch), piece(c + 2 * odd, ch), send_direct.at[ch],
                        recv.at[c + 2 * odd, ch], {"horiz": direct})
            cp.start()
            directs.append(cp)
        mates = []
        for ch in range(CHUNKS):
            cp = remote(piece(own, ch), piece(3 * c, ch), send_mate.at[ch],
                        recv.at[3 * c, ch], {"horiz": mate})
            cp.start()
            mates.append(cp)

        @pl.when(jnp.logical_not(has_adj))
        def _():
            info_adj[...] = jnp.zeros_like(info_adj)
            win[2 * c] = jnp.zeros((rows, cols), F32)
            win[2 * c + 1] = jnp.zeros((rows, cols), F32)

        @pl.when(first_slab)
        def _():
            fbuf[0:classes] = jnp.zeros((classes, 3 * cols), F32)
            pbuf[0:classes] = jnp.zeros((classes, 2 * cols), F32)

        @pl.when(last_slab)
        def _():
            fbuf[classes + rows:] = jnp.zeros((classes, 3 * cols), F32)
            pbuf[classes + rows:] = jnp.zeros((classes, 2 * cols), F32)

        def fwd_copy(i, ch):
            return remote(piece(2 * c + i, ch), piece(2 * (1 - c) + i, ch), send_fwd.at[i, ch],
                          recv.at[2 * (1 - c) + i, ch], {"horiz": fwd})

        def arrive(ch):
            for i in range(2):
                @pl.when(has_adj)
                def _():
                    remote(piece(2 * c + i, ch), piece(2 * c + i, ch), send_fwd.at[i, ch],
                           recv.at[2 * c + i, ch], {"horiz": mate}).wait_recv()

                @pl.when(has_fwd)
                def _():
                    fwd_copy(i, ch).start()

        def build(dst, source, tile):
            base = (tile - 1) * cols
            mask = source[4:5].astype(F32)
            for b in range(3):
                at = lax.broadcasted_iota(jnp.int32, (cols, cols), 0) + (base + b * cols)
                total = jnp.zeros((cols, cols), F32)
                for q in range(NB):
                    total = total + jnp.where(at == source[q:q + 1], 1.0, 0.0)
                dst[b * cols:(b + 1) * cols] = (total * mask).astype(BF)

        build(g_own, info, t)

        wide = rows + 2 * classes
        lane = lax.broadcasted_iota(jnp.int32, (classes, wide), 1)
        row = lax.broadcasted_iota(jnp.int32, (classes, wide), 0)
        prev = jnp.where(lane == row + rows, 1.0, 0.0)

        def level_of_matrix(k, prev):
            bk = binv[k]
            mhi, mlo = split(bk[:, :classes] * rate_row[k])
            qhi, qlo = split(prev)
            new = mm3(mhi, mlo, qhi, qlo)
            both = jnp.concatenate([bk] * (wide // (2 * classes)), axis=1)
            new = new + jnp.where(lax.div(lane, classes) == k, both, 0.0)
            nhi, nlo = split(new)
            phi[pl.ds(pl.multiple_of(k * classes, classes), classes)] = nhi
            plo[pl.ds(pl.multiple_of(k * classes, classes), classes)] = nlo
            return new

        for ch in range(CHUNKS):
            lo = ch * (levels // CHUNKS)
            prev = lax.fori_loop(lo, lo + levels // CHUNKS, level_of_matrix, prev)
            arrive(ch)

        @pl.when(has_adj)
        def _():
            adj_copy.wait_recv()

        build(g_adj, info_adj, adj)
        for ch in range(CHUNKS):
            remote(piece(mate_pos, ch), piece(mate_pos, ch), send_mate.at[ch],
                   recv.at[mate_pos, ch], {"horiz": mate}).wait_recv()

        def gather(src, first, g, r):
            out = jnp.zeros((block, cols), F32)
            for b in range(3):
                hi, lo = split(src[first + b, r])
                gb = g[b * cols:(b + 1) * cols]
                out = out + mm(hi, gb) + mm(lo, gb)
            return out

        def put_x(r, s, value):
            hi, lo = split(value)
            xhi[r, s * cols:(s + 1) * cols] = hi
            xlo[r, s * cols:(s + 1) * cols] = lo

        def blocks(fn):
            def step(i, carry):
                fn(pl.ds(pl.multiple_of(i * block, block), block))
                return carry
            lax.fori_loop(0, rows // block, step, 0)

        def own_first(r):
            value = gather(win, own - 1, g_own, r)
            h1[1, r] = value
            put_x(r, 0, win[own, r])
            put_x(r, 1, value)

        blocks(own_first)
        h_copy = remote(h1.at[1], h1.at[2 * c], h_s, h_r, {"horiz": mate})
        h_copy.start()

        def adj_first(r):
            h1[2 * c, r] = gather(win, c, g_adj, r)

        def second_sum(r):
            put_x(r, 2, gather(h1, 0, g_own, r))

        h_slot = 2 - 2 * c
        h_adj = 2 * c
        del h_slot, h_adj
        blocks(adj_first)
        h_copy.wait_recv()
        blocks(second_sum)

        def sweep(x_cols, buf, out, up_cols, sem):
            down = remote(out, buf.at[0:classes], v_s.at[sem], v_r.at[sem], {"vert": v + 1})
            up = remote(buf.at[classes:2 * classes, 0:up_cols],
                        buf.at[classes + rows:2 * classes + rows, 0:up_cols],
                        v_s.at[sem + 1], v_r.at[sem + 1], {"vert": v - 1})
            tail = slice(rows - classes, rows)
            last = mm3(phi[tail, :rows], plo[tail, :rows], xhi[:, :x_cols], xlo[:, :x_cols])
            out[...] = last

            @pl.when(jnp.logical_and(first_slab, slabs > 1))
            def _():
                down.start()

            for b in range(rows // block):
                r = slice(b * block, (b + 1) * block)
                k = slice(0, (b + 1) * block)
                buf[classes + b * block:classes + (b + 1) * block] = mm3(
                    phi[r, k], plo[r, k], xhi[k, :x_cols], xlo[k, :x_cols])

            @pl.when(jnp.logical_not(first_slab))
            def _():
                down.wait_recv()
                ihi, ilo = split(buf[0:classes])
                ti = slice(rows, rows + classes)
                out[...] = out[...] + mm3(phi[tail, ti], plo[tail, ti], ihi, ilo)

                @pl.when(jnp.logical_not(last_slab))
                def _():
                    down.start()

                for b in range(rows // block):
                    r = slice(b * block, (b + 1) * block)
                    br = slice(classes + b * block, classes + (b + 1) * block)
                    buf[br] = buf[br] + mm3(phi[r, ti], plo[r, ti], ihi, ilo)
                    if b == 0:
                        up.start()

            @pl.when(jnp.logical_not(last_slab))
            def _():
                up.wait_recv()
                down.wait_send()

            @pl.when(jnp.logical_not(first_slab))
            def _():
                up.wait_send()

        def operate(k, buf, width):
            at = pl.multiple_of(k * classes, classes)
            here = buf[pl.ds(at + classes, classes), 0:width]
            above = buf[pl.ds(at, classes), 0:width]
            below = buf[pl.ds(at + 2 * classes, classes), 0:width]
            chi, clo = split(coup[k])
            hhi, hlo = split(here)
            reps = width // 128
            d = jnp.concatenate([diag[pl.ds(at, classes)]] * reps, axis=1)
            ra = jnp.concatenate([rate[pl.ds(at, classes)]] * reps, axis=1)
            return (d * here + mm3(chi, clo, hhi, hlo) - ra * above - VERT_DIFFUSION * below)

        sweep(3 * cols, fbuf, fout, 2 * cols, 0)

        def middle(k, carry):
            r = pl.ds(pl.multiple_of(k * classes, classes), classes)
            rf = pl.ds(pl.multiple_of(k * classes + classes, classes), classes)
            lf = operate(k, fbuf, 2 * cols)
            m = win[own, r] - lf[:, :cols] + HORIZ_DIFFUSION * fbuf[rf, cols:2 * cols]
            hm = h1[1, r] - lf[:, cols:] + HORIZ_DIFFUSION * fbuf[rf, 2 * cols:3 * cols]
            mid[r] = m
            put_x(r, 0, m)
            put_x(r, 1, hm)
            return carry

        lax.fori_loop(0, levels, middle, 0)
        sweep(2 * cols, pbuf, pout, cols, 2)
        sbuf[...] = CA * fbuf[:, 0:cols] + CB * pbuf[:, 0:cols]

        def final(k, carry):
            r = pl.ds(pl.multiple_of(k * classes, classes), classes)
            rf = pl.ds(pl.multiple_of(k * classes + classes, classes), classes)
            hs = CA * fbuf[rf, cols:2 * cols] + CB * pbuf[rf, cols:2 * cols]
            sol[r] = fbuf[rf, 0:cols] + sbuf[rf]
            res[r] = mid[r] - operate(k, sbuf, cols) + HORIZ_DIFFUSION * hs
            return carry

        lax.fori_loop(0, levels, final, 0)

        for cp in directs + mates:
            cp.wait_send()
        h_copy.wait_send()

        @pl.when(has_adj)
        def _():
            adj_copy.wait_send()

        @pl.when(has_fwd)
        def _():
            for ch in range(CHUNKS):
                for i in range(2):
                    fwd_copy(i, ch).wait_send()

    return kernel


def solution(mesh):
    tiles, slabs = mesh.shape["horiz"], mesh.shape["vert"]

    def body(right_side, neighbours, ocean_count, settling, coupling, precond_inverse):
        levels, classes, cols = right_side.shape
        rows = levels * classes
        start = lax.axis_index("vert") * levels
        inflow = jnp.concatenate([jnp.zeros_like(settling[:1]), settling[:-1]], 0) + VERT_DIFFUSION
        rate = lax.dynamic_slice_in_dim(inflow, start, levels, 0)
        diag = (1.0 + lax.dynamic_slice_in_dim(settling, start, levels, 0)
                + 2.0 * VERT_DIFFUSION + NB * HORIZ_DIFFUSION)
        twice = jnp.concatenate([precond_inverse] * 2, axis=2)
        spread = lambda x: jnp.broadcast_to(x.reshape(rows, 1), (rows, 128))
        vm = pl.BlockSpec(memory_space=pltpu.VMEM)
        dma = pltpu.SemaphoreType.DMA
        wide = rows + 2 * classes
        sol, res = pl.pallas_call(
            make_kernel(tiles, slabs, levels, classes, cols),
            out_shape=[jax.ShapeDtypeStruct((rows, cols), F32)] * 2,
            in_specs=[vm, vm, pl.BlockSpec(memory_space=pltpu.SMEM)] + [vm] * 5,
            out_specs=[vm, vm],
            scratch_shapes=[
                pltpu.VMEM((4, rows, cols), F32),
                pltpu.VMEM((8, cols), jnp.int32),
                pltpu.VMEM((8, cols), jnp.int32),
                pltpu.VMEM((3, rows, cols), F32),
                pltpu.VMEM((3 * cols, cols), BF),
                pltpu.VMEM((3 * cols, cols), BF),
                pltpu.VMEM((rows, wide), BF),
                pltpu.VMEM((rows, wide), BF),
                pltpu.VMEM((rows, 3 * cols), BF),
                pltpu.VMEM((rows, 3 * cols), BF),
                pltpu.VMEM((rows + 2 * classes, 3 * cols), F32),
                pltpu.VMEM((classes, 3 * cols), F32),
                pltpu.VMEM((rows, cols), F32),
                pltpu.VMEM((rows + 2 * classes, 2 * cols), F32),
                pltpu.VMEM((classes, 2 * cols), F32),
                pltpu.VMEM((rows + 2 * classes, cols), F32),
                dma((4, CHUNKS)), dma((CHUNKS,)), dma((CHUNKS,)), dma((2, CHUNKS)),
                dma, dma, dma, dma, dma((4,)), dma((4,)),
            ],
            compiler_params=pltpu.CompilerParams(
                has_side_effects=True, vmem_limit_bytes=56 * 2**20),
            name="settle",
        )(right_side.reshape(rows, cols), neighbours, ocean_count, twice, coupling,
          rate.reshape(levels, 1, classes), spread(diag), spread(rate))
        return sol.reshape(right_side.shape), res.reshape(right_side.shape)

    in_specs = (P("vert", None, "horiz"), P(None, "horiz"), P("horiz"), P(),
                P("vert", None, None), P("vert", None, None))
    out_specs = (P("vert", None, "horiz"), P("vert", None, "horiz"))
    return jax.shard_map(body, mesh=mesh, in_specs=in_specs, out_specs=out_specs, check_vma=False)
```

time: 236 us -> 84.4 us (0.36)
  the two profiles are of different devices: /device:TPU:14 before, /device:TPU:12 now
where the time goes in v1:
time: 84.4 us; the launch traced here: 82.9 us
  Pallas kernels  74.5 us (88%)
  local copies, waits for them, and re-layouts  6.06 us (7%)
  between operations  1.33 us (2%)
  other arithmetic  1.01 us (1%)
    pallas_call x1, Pallas kernels, body(): pl.pallas_call(make_kernel(tiles, slabs, levels, classes, cols), out_shap...  74.5 us
    unnamed x10, local copies, waits for them, and re-layouts  3.94 us
    broadcast_in_dim x4, local copies, waits for them, and re-layouts, body(): spread = lambda x: jnp.broadcast_to(x.reshape(rows, 1), (rows, 128))  2.12 us

profile of v1, /device:TPU:12, one launch (start us, length us, event | category | flops | bytes accessed | tf_op | source)
XLA Modules:
  0.0 82.9 jit_solution(13458146448291854926)
XLA Ops:
  0.6 0.0 copy-start.3
  1.3 0.0 copy-done.3
  1.4 0.0 copy-start.2
  1.4 0.1 broadcast_in_dim.15
  1.4 0.5 copy-done.2
  2.0 0.1 broadcast_in_dim.17
  2.0 0.0 copy-start.1
  2.0 1.0 %broadcast_in_dim.18.rate = f32[1024,128]{1,0:T(8,128)} broadcast(f32[1024]{0:T(1024)S(1)} %broadcast_in_dim.17), dimensions={0} | broadcast | bytes 528384 | tf_op jit(solution)/shard_map/broadcast_in_dim | solution.py:329
  3.0 1.0 %broadcast_in_dim.16.diag = f32[1024,128]{1,0:T(8,128)} broadcast(f32[1024]{0:T(1024)S(1)} %broadcast_in_dim.15), dimensions={0} | broadcast | bytes 528384 | tf_op jit(solution)/shard_map/broadcast_in_dim | solution.py:329
  4.0 0.0 copy-done.1
  4.0 1.0 %pad_maximum_fusion.binv = f32[16,64,128]{2,1,0:T(8,128)} fusion(f32[16,64,64]{2,1,0:T(8,128)S(1)} %copy-done.1), kind=kLoop, calls=%fused_computation | loop fusion | flops 131072 | bytes 786432 | tf_op jit(solution)/shard_map/concatenate | solution.py:328
  5.0 74.5 %settle.1 = (f32[1024,256]{1,0:T(8,128)}, f32[1024,256]{1,0:T(8,128)}) custom-call(f32[1024,256]{1,0:T(8,128)} %bitcast.7, s32[4,256]{1,0:T(4,128)} %nbr.1, s32[1]{0:T(128)S(6)} %copy.10.count, f32[16,64,128]{2,1,0:T(8,128)} %pad_maximum_fusion.binv, f32[16,64,64]{2,1,0:T(8,128)} %coup.1, f32[16,1,64]{2,1,0:T(1,128)} %bitcast.8, ...), custom_call_target="tpu_custom_call" | custom-call | tf_op jit(solution)/shard_map/settle/pallas_call | solution.py:333
  79.5 0.0 copy-start
  79.5 2.4 %copy.11 = f32[16,64,256]{2,1,0:T(8,128)} copy(f32[16,64,256]{2,1,0:T(8,128)} %bitcast.6) | data formatting | bytes 2097152
  81.9 0.0 copy-done
  81.9 1.0 %copy.12 = f32[16,64,256]{2,1,0:T(8,128)} copy(f32[16,64,256]{2,1,0:T(8,128)S(1)} %bitcast.5) | data formatting | bytes 2097152
  (1 shorter events, 0.0 us)
Async XLA Ops:
  0.6 0.7 copy-start.3
  1.4 0.6 copy-start.2
  2.0 2.0 %copy-start.1 = (f32[16,64,64]{2,1,0:T(8,128)S(1)}, f32[16,64,64]{2,1,0:T(8,128)}, u32[]{:S(2)}) copy-start(f32[16,64,64]{2,1,0:T(8,128)} %param.11) | copy-start | bytes 786436
  79.5 2.4 %copy-start = (f32[1024,256]{1,0:T(8,128)S(1)}, f32[1024,256]{1,0:T(8,128)}, u32[]{:S(2)}) copy-start(f32[1024,256]{1,0:T(8,128)} %get-tuple-element.5) | copy-start | bytes 3145732

commit v2 on v1

--- a/solution.py
+++ b/solution.py
@@ -17,7 +17,7 @@
 
 F32 = jnp.float32
 BF = jnp.bfloat16
-CHUNKS = 4
+CHUNKS = 8
 
 
 def split(x):
@@ -38,7 +38,7 @@
     part = rows // CHUNKS
     block = 256
 
-    def kernel(rhs, nbr, count, binv, coup, rate_row, diag, rate, sol, res,
+    def kernel(rhs, nbr, count, settling, coup, binv, sol, res,
                win, info, info_adj, h1, g_own, g_adj, phi, plo, xhi, xlo, fbuf, fout, mid,
                pbuf, pout, sbuf,
                recv, send_mate, send_direct, send_fwd, info_s, info_r, h_s, h_r, v_s, v_r):
@@ -67,6 +67,45 @@
         def piece(pos, ch):
             return win.at[pos, pl.ds(ch * part, part)]
 
+        pj = j + 1 - 2 * odd
+        partner_inner = direct
+        partner_outer = 4 * pj + 1 - direct
+        outer = jnp.logical_not(inner)
+        from_fwd = jnp.where(odd == 0, 2 * j - 3, 2 * j + 4)
+        outer_adj = jnp.logical_and(outer, has_adj)
+        barrier = pltpu.get_barrier_semaphore()
+
+        def greet(to):
+            pl.semaphore_signal(barrier, inc=1, device_id=to, device_id_type=pl.DeviceIdType.MESH)
+
+        greet({"horiz": mate})
+        greet({"horiz": partner_inner})
+
+        @pl.when(inner)
+        def _():
+            greet({"horiz": partner_outer})
+
+        @pl.when(has_fwd)
+        def _():
+            greet({"horiz": fwd})
+
+        @pl.when(outer_adj)
+        def _():
+            greet({"horiz": from_fwd})
+            greet({"horiz": adj})
+
+        @pl.when(jnp.logical_not(first_slab))
+        def _():
+            greet({"vert": v - 1})
+
+        @pl.when(jnp.logical_not(last_slab))
+        def _():
+            greet({"vert": v + 1})
+
+        greeted = (2 + jnp.where(inner, 1, 0) + jnp.where(has_fwd, 1, 0)
+                   + jnp.where(outer_adj, 2, 0) + jnp.where(first_slab, 0, 1)
+                   + jnp.where(last_slab, 0, 1))
+
         inside = lax.broadcasted_iota(jnp.int32, (1, cols), 1)
         n = count[0]
         low = lax.div(n + 1, 2)
@@ -75,16 +114,18 @@
         ocean_i = ocean.astype(jnp.int32)
         ocean_f = ocean.astype(F32)
         info[...] = jnp.concatenate([nbr[...], jnp.broadcast_to(ocean_i, (4, cols))], axis=0)
-        adj_copy = remote(info, info_adj, info_s, info_r, {"horiz": adj})
-
-        @pl.when(has_adj)
-        def _():
-            adj_copy.start()
-
-        directs = []
         for ch in range(CHUNKS):
             r = pl.ds(ch * part, part)
             win[own, r] = rhs[r] * ocean_f
+        pl.semaphore_wait(barrier, greeted)
+        adj_copy = remote(info, info_adj, info_s, info_r, {"horiz": adj})
+
+        @pl.when(has_adj)
+        def _():
+            adj_copy.start()
+
+        directs = []
+        for ch in range(CHUNKS):
             cp = remote(piece(own, ch), piece(c + 2 * odd, ch), send_direct.at[ch],
                         recv.at[c + 2 * odd, ch], {"horiz": direct})
             cp.start()
@@ -139,6 +180,21 @@
 
         build(g_own, info, t)
 
+        eye = (lax.broadcasted_iota(jnp.int32, (classes, classes), 0)
+               == lax.broadcasted_iota(jnp.int32, (classes, classes), 1))
+
+        def rate_of(k):
+            level = v * levels + k
+            above = settling[pl.ds(jnp.maximum(level - 1, 0), 1)]
+            return jnp.where(level > 0, above, 0.0) + VERT_DIFFUSION
+
+        def diag_of(k):
+            return (1.0 + settling[pl.ds(v * levels + k, 1)] + 2.0 * VERT_DIFFUSION
+                    + NB * HORIZ_DIFFUSION)
+
+        def column(x):
+            return jnp.sum(jnp.where(eye, x, 0.0), axis=1, keepdims=True)
+
         wide = rows + 2 * classes
         lane = lax.broadcasted_iota(jnp.int32, (classes, wide), 1)
         row = lax.broadcasted_iota(jnp.int32, (classes, wide), 0)
@@ -146,29 +202,24 @@
 
         def level_of_matrix(k, prev):
             bk = binv[k]
-            mhi, mlo = split(bk[:, :classes] * rate_row[k])
+            mhi, mlo = split(bk * rate_of(k))
             qhi, qlo = split(prev)
             new = mm3(mhi, mlo, qhi, qlo)
-            both = jnp.concatenate([bk] * (wide // (2 * classes)), axis=1)
+            both = jnp.concatenate([bk, bk], axis=1)
+            both = jnp.concatenate([both] * (wide // (2 * classes)), axis=1)
             new = new + jnp.where(lax.div(lane, classes) == k, both, 0.0)
             nhi, nlo = split(new)
             phi[pl.ds(pl.multiple_of(k * classes, classes), classes)] = nhi
             plo[pl.ds(pl.multiple_of(k * classes, classes), classes)] = nlo
             return new
 
-        for ch in range(CHUNKS):
-            lo = ch * (levels // CHUNKS)
-            prev = lax.fori_loop(lo, lo + levels // CHUNKS, level_of_matrix, prev)
-            arrive(ch)
+        lax.fori_loop(0, levels, level_of_matrix, prev)
 
         @pl.when(has_adj)
         def _():
             adj_copy.wait_recv()
 
         build(g_adj, info_adj, adj)
-        for ch in range(CHUNKS):
-            remote(piece(mate_pos, ch), piece(mate_pos, ch), send_mate.at[ch],
-                   recv.at[mate_pos, ch], {"horiz": mate}).wait_recv()
 
         def gather(src, first, g, r):
             out = jnp.zeros((block, cols), F32)
@@ -183,66 +234,71 @@
             xhi[r, s * cols:(s + 1) * cols] = hi
             xlo[r, s * cols:(s + 1) * cols] = lo
 
-        def blocks(fn):
-            def step(i, carry):
-                fn(pl.ds(pl.multiple_of(i * block, block), block))
-                return carry
-            lax.fori_loop(0, rows // block, step, 0)
-
-        def own_first(r):
+        tail = slice(rows - classes, rows)
+        ti = slice(rows, rows + classes)
+        n_blocks = rows // block
+
+        def first_sums(b):
+            r = slice(b * block, (b + 1) * block)
             value = gather(win, own - 1, g_own, r)
             h1[1, r] = value
             put_x(r, 0, win[own, r])
             put_x(r, 1, value)
-
-        blocks(own_first)
-        h_copy = remote(h1.at[1], h1.at[2 * c], h_s, h_r, {"horiz": mate})
-        h_copy.start()
-
-        def adj_first(r):
+            h_copy[b].start()
             h1[2 * c, r] = gather(win, c, g_adj, r)
 
-        def second_sum(r):
+        def sweep_block(b, x_cols, buf):
+            r = slice(b * block, (b + 1) * block)
+            k = slice(0, (b + 1) * block)
+            buf[classes + b * block:classes + (b + 1) * block] = mm3(
+                phi[r, k], plo[r, k], xhi[k, :x_cols], xlo[k, :x_cols])
+
+        def second_sums(b):
+            r = slice(b * block, (b + 1) * block)
+            h_copy[b].wait_recv()
             put_x(r, 2, gather(h1, 0, g_own, r))
-
-        h_slot = 2 - 2 * c
-        h_adj = 2 * c
-        del h_slot, h_adj
-        blocks(adj_first)
-        h_copy.wait_recv()
-        blocks(second_sum)
-
-        def sweep(x_cols, buf, out, up_cols, sem):
+            sweep_block(b, 3 * cols, fbuf)
+
+        h_copy = []
+        for b in range(n_blocks):
+            r = pl.ds(b * block, block)
+            h_copy.append(remote(h1.at[1, r], h1.at[2 * c, r], h_s.at[b], h_r.at[b],
+                                 {"horiz": mate}))
+        per = CHUNKS // n_blocks
+        for b in range(n_blocks):
+            for ch in range(b * per, (b + 1) * per):
+                remote(piece(mate_pos, ch), piece(mate_pos, ch), send_mate.at[ch],
+                       recv.at[mate_pos, ch], {"horiz": mate}).wait_recv()
+                arrive(ch)
+            first_sums(b)
+            if b > 0:
+                second_sums(b - 1)
+        second_sums(n_blocks - 1)
+
+        def relay(buf, out, up_cols, sem, rest):
             down = remote(out, buf.at[0:classes], v_s.at[sem], v_r.at[sem], {"vert": v + 1})
             up = remote(buf.at[classes:2 * classes, 0:up_cols],
                         buf.at[classes + rows:2 * classes + rows, 0:up_cols],
                         v_s.at[sem + 1], v_r.at[sem + 1], {"vert": v - 1})
-            tail = slice(rows - classes, rows)
-            last = mm3(phi[tail, :rows], plo[tail, :rows], xhi[:, :x_cols], xlo[:, :x_cols])
-            out[...] = last
+            out[...] = buf[rows:rows + classes]
 
             @pl.when(jnp.logical_and(first_slab, slabs > 1))
             def _():
                 down.start()
 
-            for b in range(rows // block):
-                r = slice(b * block, (b + 1) * block)
-                k = slice(0, (b + 1) * block)
-                buf[classes + b * block:classes + (b + 1) * block] = mm3(
-                    phi[r, k], plo[r, k], xhi[k, :x_cols], xlo[k, :x_cols])
+            rest()
 
             @pl.when(jnp.logical_not(first_slab))
             def _():
                 down.wait_recv()
                 ihi, ilo = split(buf[0:classes])
-                ti = slice(rows, rows + classes)
                 out[...] = out[...] + mm3(phi[tail, ti], plo[tail, ti], ihi, ilo)
 
                 @pl.when(jnp.logical_not(last_slab))
                 def _():
                     down.start()
 
-                for b in range(rows // block):
+                for b in range(n_blocks):
                     r = slice(b * block, (b + 1) * block)
                     br = slice(classes + b * block, classes + (b + 1) * block)
                     buf[br] = buf[br] + mm3(phi[r, ti], plo[r, ti], ihi, ilo)
@@ -265,12 +321,11 @@
             below = buf[pl.ds(at + 2 * classes, classes), 0:width]
             chi, clo = split(coup[k])
             hhi, hlo = split(here)
-            reps = width // 128
-            d = jnp.concatenate([diag[pl.ds(at, classes)]] * reps, axis=1)
-            ra = jnp.concatenate([rate[pl.ds(at, classes)]] * reps, axis=1)
+            d = column(diag_of(k))
+            ra = column(rate_of(k))
             return (d * here + mm3(chi, clo, hhi, hlo) - ra * above - VERT_DIFFUSION * below)
 
-        sweep(3 * cols, fbuf, fout, 2 * cols, 0)
+        relay(fbuf, fout, 2 * cols, 0, lambda: None)
 
         def middle(k, carry):
             r = pl.ds(pl.multiple_of(k * classes, classes), classes)
@@ -283,8 +338,19 @@
             put_x(r, 1, hm)
             return carry
 
-        lax.fori_loop(0, levels, middle, 0)
-        sweep(2 * cols, pbuf, pout, cols, 2)
+        def middles(i, carry):
+            for u in range(4):
+                middle(4 * i + u, carry)
+            return carry
+
+        lax.fori_loop(0, levels // 4, middles, 0)
+        sweep_block(n_blocks - 1, 2 * cols, pbuf)
+
+        def others():
+            for b in range(n_blocks - 1):
+                sweep_block(b, 2 * cols, pbuf)
+
+        relay(pbuf, pout, cols, 2, others)
         sbuf[...] = CA * fbuf[:, 0:cols] + CB * pbuf[:, 0:cols]
 
         def final(k, carry):
@@ -295,11 +361,17 @@
             res[r] = mid[r] - operate(k, sbuf, cols) + HORIZ_DIFFUSION * hs
             return carry
 
-        lax.fori_loop(0, levels, final, 0)
+        def finals(i, carry):
+            for u in range(4):
+                final(4 * i + u, carry)
+            return carry
+
+        lax.fori_loop(0, levels // 4, finals, 0)
 
         for cp in directs + mates:
             cp.wait_send()
-        h_copy.wait_send()
+        for cp in h_copy:
+            cp.wait_send()
 
         @pl.when(has_adj)
         def _():
@@ -320,20 +392,13 @@
     def body(right_side, neighbours, ocean_count, settling, coupling, precond_inverse):
         levels, classes, cols = right_side.shape
         rows = levels * classes
-        start = lax.axis_index("vert") * levels
-        inflow = jnp.concatenate([jnp.zeros_like(settling[:1]), settling[:-1]], 0) + VERT_DIFFUSION
-        rate = lax.dynamic_slice_in_dim(inflow, start, levels, 0)
-        diag = (1.0 + lax.dynamic_slice_in_dim(settling, start, levels, 0)
-                + 2.0 * VERT_DIFFUSION + NB * HORIZ_DIFFUSION)
-        twice = jnp.concatenate([precond_inverse] * 2, axis=2)
-        spread = lambda x: jnp.broadcast_to(x.reshape(rows, 1), (rows, 128))
         vm = pl.BlockSpec(memory_space=pltpu.VMEM)
         dma = pltpu.SemaphoreType.DMA
         wide = rows + 2 * classes
         sol, res = pl.pallas_call(
             make_kernel(tiles, slabs, levels, classes, cols),
             out_shape=[jax.ShapeDtypeStruct((rows, cols), F32)] * 2,
-            in_specs=[vm, vm, pl.BlockSpec(memory_space=pltpu.SMEM)] + [vm] * 5,
+            in_specs=[vm, vm, pl.BlockSpec(memory_space=pltpu.SMEM)] + [vm] * 3,
             out_specs=[vm, vm],
             scratch_shapes=[
                 pltpu.VMEM((4, rows, cols), F32),
@@ -353,13 +418,13 @@
                 pltpu.VMEM((classes, 2 * cols), F32),
                 pltpu.VMEM((rows + 2 * classes, cols), F32),
                 dma((4, CHUNKS)), dma((CHUNKS,)), dma((CHUNKS,)), dma((2, CHUNKS)),
-                dma, dma, dma, dma, dma((4,)), dma((4,)),
+                dma, dma, dma((4,)), dma((4,)), dma((4,)), dma((4,)),
             ],
             compiler_params=pltpu.CompilerParams(
-                has_side_effects=True, vmem_limit_bytes=56 * 2**20),
+                collective_id=0, has_side_effects=True, vmem_limit_bytes=56 * 2**20),
             name="settle",
-        )(right_side.reshape(rows, cols), neighbours, ocean_count, twice, coupling,
-          rate.reshape(levels, 1, classes), spread(diag), spread(rate))
+        )(right_side.reshape(rows, cols), neighbours, ocean_count, settling, coupling,
+          precond_inverse)
         return sol.reshape(right_side.shape), res.reshape(right_side.shape)
 
     in_specs = (P("vert", None, "horiz"), P(None, "horiz"), P("horiz"), P(),

time: 84.4 us -> 69.4 us (0.82); the launches traced: 82.9 us -> 69.2 us
  Pallas kernels: 74.5 us -> 64.6 us
  local copies, waits for them, and re-layouts: 6.06 us -> 3.36 us
  other arithmetic: 1.01 us -> 0 us
    pallas_call x1, Pallas kernels: 74.5 us -> 64.6 us  [body(): pl.pallas_call(make_kernel(tiles, slabs, levels, classes, cols), out_shap...]
    broadcast_in_dim x4 -> x0, local copies, waits for them, and re-layouts: 2.12 us -> none  [body(): spread = lambda x: jnp.broadcast_to(x.reshape(rows, 1), (rows, 128))]
    concatenate x1 -> x0, other arithmetic: 1 us -> none  [body(): twice = jnp.concatenate([precond_inverse] * 2, axis=2)]
    unnamed x10 -> x4, local copies, waits for them, and re-layouts: 3.94 us -> 3.36 us
where the time goes in v2:
time: 69.4 us; the launch traced here: 69.2 us
  Pallas kernels  64.6 us (93%)
  local copies, waits for them, and re-layouts  3.36 us (5%)
  between operations  1.29 us (2%)
    pallas_call x1, Pallas kernels, body(): pl.pallas_call(make_kernel(tiles, slabs, levels, classes, cols), out_shap...  64.6 us
    unnamed x4, local copies, waits for them, and re-layouts  3.36 us

profile of v2, /device:TPU:12, one launch (start us, length us, event | category | flops | bytes accessed | tf_op | source)
XLA Modules:
  0.0 69.2 jit_solution(15233086894481833494)
XLA Ops:
  1.3 64.6 %settle.1 = (f32[1024,256]{1,0:T(8,128)}, f32[1024,256]{1,0:T(8,128)}) custom-call(f32[1024,256]{1,0:T(8,128)} %bitcast.3, s32[4,256]{1,0:T(4,128)} %nbr.1, s32[1]{0:T(128)S(6)} %copy.10.count, f32[32,64]{1,0:T(8,128)} %settling.1, f32[16,64,64]{2,1,0:T(8,128)} %coup.1, f32[16,64,64]{2,1,0:T(8,128)} %binv.1), custom_call_target="tpu_custom_call" | custom-call | tf_op jit(solution)/shard_map/settle/pallas_call | solution.py:398
  65.9 0.0 copy-start
  65.9 2.4 %copy.11 = f32[16,64,256]{2,1,0:T(8,128)} copy(f32[16,64,256]{2,1,0:T(8,128)} %bitcast.5) | data formatting | bytes 2097152
  68.3 0.0 copy-done
  68.3 1.0 %copy.12 = f32[16,64,256]{2,1,0:T(8,128)} copy(f32[16,64,256]{2,1,0:T(8,128)S(1)} %bitcast.4) | data formatting | bytes 2097152
Async XLA Ops:
  65.9 2.4 %copy-start = (f32[1024,256]{1,0:T(8,128)S(1)}, f32[1024,256]{1,0:T(8,128)}, u32[]{:S(2)}) copy-start(f32[1024,256]{1,0:T(8,128)} %get-tuple-element.5) | copy-start | bytes 3145732

commit v3 on v2

--- a/solution.py
+++ b/solution.py
@@ -17,7 +17,7 @@
 
 F32 = jnp.float32
 BF = jnp.bfloat16
-CHUNKS = 8
+CHUNKS = 16
 
 
 def split(x):
@@ -213,7 +213,11 @@
             plo[pl.ds(pl.multiple_of(k * classes, classes), classes)] = nlo
             return new
 
-        lax.fori_loop(0, levels, level_of_matrix, prev)
+        early = CHUNKS // 4
+        for ch in range(early):
+            lo, hi = levels * ch // early, levels * (ch + 1) // early
+            prev = lax.fori_loop(lo, hi, level_of_matrix, prev)
+            arrive(ch)
 
         @pl.when(has_adj)
         def _():
@@ -269,7 +273,8 @@
             for ch in range(b * per, (b + 1) * per):
                 remote(piece(mate_pos, ch), piece(mate_pos, ch), send_mate.at[ch],
                        recv.at[mate_pos, ch], {"horiz": mate}).wait_recv()
-                arrive(ch)
+                if ch >= early:
+                    arrive(ch)
             first_sums(b)
             if b > 0:
                 second_sums(b - 1)
@@ -305,17 +310,20 @@
                     if b == 0:
                         up.start()
 
-            @pl.when(jnp.logical_not(last_slab))
-            def _():
-                up.wait_recv()
-                down.wait_send()
-
-            @pl.when(jnp.logical_not(first_slab))
-            def _():
-                up.wait_send()
+            def finish():
+                @pl.when(jnp.logical_not(last_slab))
+                def _():
+                    up.wait_recv()
+                    down.wait_send()
+
+                @pl.when(jnp.logical_not(first_slab))
+                def _():
+                    up.wait_send()
+
+            return finish
 
         def operate(k, buf, width):
-            at = pl.multiple_of(k * classes, classes)
+            at = k * classes if isinstance(k, int) else pl.multiple_of(k * classes, classes)
             here = buf[pl.ds(at + classes, classes), 0:width]
             above = buf[pl.ds(at, classes), 0:width]
             below = buf[pl.ds(at + 2 * classes, classes), 0:width]
@@ -325,11 +333,15 @@
             ra = column(rate_of(k))
             return (d * here + mm3(chi, clo, hhi, hlo) - ra * above - VERT_DIFFUSION * below)
 
-        relay(fbuf, fout, 2 * cols, 0, lambda: None)
+        finish_f = relay(fbuf, fout, 2 * cols, 0, lambda: None)
+
+        def level_rows(k, more):
+            at = (k + more) * classes
+            return pl.ds(at if isinstance(k, int) else pl.multiple_of(at, classes), classes)
 
         def middle(k, carry):
-            r = pl.ds(pl.multiple_of(k * classes, classes), classes)
-            rf = pl.ds(pl.multiple_of(k * classes + classes, classes), classes)
+            r = level_rows(k, 0)
+            rf = level_rows(k, 1)
             lf = operate(k, fbuf, 2 * cols)
             m = win[own, r] - lf[:, :cols] + HORIZ_DIFFUSION * fbuf[rf, cols:2 * cols]
             hm = h1[1, r] - lf[:, cols:] + HORIZ_DIFFUSION * fbuf[rf, 2 * cols:3 * cols]
@@ -343,19 +355,23 @@
                 middle(4 * i + u, carry)
             return carry
 
-        lax.fori_loop(0, levels // 4, middles, 0)
+        lax.fori_loop(0, levels // 4 - 1, middles, 0)
+        finish_f()
+        middles(levels // 4 - 1, 0)
         sweep_block(n_blocks - 1, 2 * cols, pbuf)
 
         def others():
             for b in range(n_blocks - 1):
                 sweep_block(b, 2 * cols, pbuf)
 
-        relay(pbuf, pout, cols, 2, others)
-        sbuf[...] = CA * fbuf[:, 0:cols] + CB * pbuf[:, 0:cols]
+        finish_p = relay(pbuf, pout, cols, 2, others)
+        upper = slice(0, classes + rows)
+        below_row = slice(classes + rows, 2 * classes + rows)
+        sbuf[upper] = CA * fbuf[upper, 0:cols] + CB * pbuf[upper, 0:cols]
 
         def final(k, carry):
-            r = pl.ds(pl.multiple_of(k * classes, classes), classes)
-            rf = pl.ds(pl.multiple_of(k * classes + classes, classes), classes)
+            r = level_rows(k, 0)
+            rf = level_rows(k, 1)
             hs = CA * fbuf[rf, cols:2 * cols] + CB * pbuf[rf, cols:2 * cols]
             sol[r] = fbuf[rf, 0:cols] + sbuf[rf]
             res[r] = mid[r] - operate(k, sbuf, cols) + HORIZ_DIFFUSION * hs
@@ -366,7 +382,10 @@
                 final(4 * i + u, carry)
             return carry
 
-        lax.fori_loop(0, levels // 4, finals, 0)
+        lax.fori_loop(0, levels // 4 - 1, finals, 0)
+        finish_p()
+        sbuf[below_row] = CA * fbuf[below_row, 0:cols] + CB * pbuf[below_row, 0:cols]
+        finals(levels // 4 - 1, 0)
 
         for cp in directs + mates:
             cp.wait_send()

time: 69.4 us -> 66.2 us (0.954)
  Pallas kernels: 64.6 us -> 61.4 us
    pallas_call x1, Pallas kernels: 64.6 us -> 61.4 us  [body(): pl.pallas_call(make_kernel(tiles, slabs, levels, classes, cols), out_shap...]
where the time goes in v3:
time: 66.2 us; the launch traced here: 66 us
  Pallas kernels  61.4 us (93%)
  local copies, waits for them, and re-layouts  3.36 us (5%)
  between operations  1.29 us (2%)
    pallas_call x1, Pallas kernels, body(): pl.pallas_call(make_kernel(tiles, slabs, levels, classes, cols), out_shap...  61.4 us
    unnamed x4, local copies, waits for them, and re-layouts  3.36 us

profile of v3, /device:TPU:12, one launch (start us, length us, event | category | flops | bytes accessed | tf_op | source)
XLA Modules:
  0.0 66.0 jit_solution(6697283168167129843)
XLA Ops:
  1.3 61.4 %settle.1 = (f32[1024,256]{1,0:T(8,128)}, f32[1024,256]{1,0:T(8,128)}) custom-call(f32[1024,256]{1,0:T(8,128)} %bitcast.3, s32[4,256]{1,0:T(4,128)} %nbr.1, s32[1]{0:T(128)S(6)} %copy.10.count, f32[32,64]{1,0:T(8,128)} %settling.1, f32[16,64,64]{2,1,0:T(8,128)} %coup.1, f32[16,64,64]{2,1,0:T(8,128)} %binv.1), custom_call_target="tpu_custom_call" | custom-call | tf_op jit(solution)/shard_map/settle/pallas_call | solution.py:417
  62.7 0.0 copy-start
  62.7 2.4 %copy.11 = f32[16,64,256]{2,1,0:T(8,128)} copy(f32[16,64,256]{2,1,0:T(8,128)} %bitcast.5) | data formatting | bytes 2097152
  65.0 0.0 copy-done
  65.0 1.0 %copy.12 = f32[16,64,256]{2,1,0:T(8,128)} copy(f32[16,64,256]{2,1,0:T(8,128)S(1)} %bitcast.4) | data formatting | bytes 2097152
Async XLA Ops:
  62.7 2.4 %copy-start = (f32[1024,256]{1,0:T(8,128)S(1)}, f32[1024,256]{1,0:T(8,128)}, u32[]{:S(2)}) copy-start(f32[1024,256]{1,0:T(8,128)} %get-tuple-element.5) | copy-start | bytes 3145732

commit v4 on v3

--- a/solution.py
+++ b/solution.py
@@ -251,17 +251,19 @@
             h_copy[b].start()
             h1[2 * c, r] = gather(win, c, g_adj, r)
 
-        def sweep_block(b, x_cols, buf):
+        def sweep_block(b, x_cols, buf, from_col=0):
             r = slice(b * block, (b + 1) * block)
             k = slice(0, (b + 1) * block)
-            buf[classes + b * block:classes + (b + 1) * block] = mm3(
-                phi[r, k], plo[r, k], xhi[k, :x_cols], xlo[k, :x_cols])
+            w = slice(from_col, x_cols)
+            buf[classes + b * block:classes + (b + 1) * block, w] = mm3(
+                phi[r, k], plo[r, k], xhi[k, w], xlo[k, w])
 
         def second_sums(b):
             r = slice(b * block, (b + 1) * block)
+            sweep_block(b, 2 * cols, fbuf)
             h_copy[b].wait_recv()
             put_x(r, 2, gather(h1, 0, g_own, r))
-            sweep_block(b, 3 * cols, fbuf)
+            sweep_block(b, 3 * cols, fbuf, 2 * cols)
 
         h_copy = []
         for b in range(n_blocks):

time: 66.2 us -> 65.1 us (0.983)
  Pallas kernels: 61.4 us -> 60.3 us
    pallas_call x1, Pallas kernels: 61.4 us -> 60.3 us  [body(): pl.pallas_call(make_kernel(tiles, slabs, levels, classes, cols), out_shap...]
where the time goes in v4:
time: 65.1 us; the launch traced here: 64.9 us
  Pallas kernels  60.3 us (93%)
  local copies, waits for them, and re-layouts  3.36 us (5%)
  between operations  1.29 us (2%)
    pallas_call x1, Pallas kernels, body(): pl.pallas_call(make_kernel(tiles, slabs, levels, classes, cols), out_shap...  60.3 us
    unnamed x4, local copies, waits for them, and re-layouts  3.36 us

profile of v4, /device:TPU:12, one launch (start us, length us, event | category | flops | bytes accessed | tf_op | source)
XLA Modules:
  0.0 64.9 jit_solution(4166906466290388264)
XLA Ops:
  1.3 60.3 %settle.1 = (f32[1024,256]{1,0:T(8,128)}, f32[1024,256]{1,0:T(8,128)}) custom-call(f32[1024,256]{1,0:T(8,128)} %bitcast.3, s32[4,256]{1,0:T(4,128)} %nbr.1, s32[1]{0:T(128)S(6)} %copy.10.count, f32[32,64]{1,0:T(8,128)} %settling.1, f32[16,64,64]{2,1,0:T(8,128)} %coup.1, f32[16,64,64]{2,1,0:T(8,128)} %binv.1), custom_call_target="tpu_custom_call" | custom-call | tf_op jit(solution)/shard_map/settle/pallas_call | solution.py:419
  61.5 0.0 copy-start
  61.6 2.4 %copy.11 = f32[16,64,256]{2,1,0:T(8,128)} copy(f32[16,64,256]{2,1,0:T(8,128)} %bitcast.5) | data formatting | bytes 2097152
  63.9 0.0 copy-done
  63.9 1.0 %copy.12 = f32[16,64,256]{2,1,0:T(8,128)} copy(f32[16,64,256]{2,1,0:T(8,128)S(1)} %bitcast.4) | data formatting | bytes 2097152
Async XLA Ops:
  61.5 2.4 %copy-start = (f32[1024,256]{1,0:T(8,128)S(1)}, f32[1024,256]{1,0:T(8,128)}, u32[]{:S(2)}) copy-start(f32[1024,256]{1,0:T(8,128)} %get-tuple-element.5) | copy-start | bytes 3145732
